TPU v7x, 32 devices: a whole 2x2x4 slice. The times are simulated.
32 devices in a mesh: segment: 2 (over core), et: 16 (over z, y, x).
Axes of the slice: x: 2, y: 2, z: 4, core: 2. Of those that a mesh axis runs over, the one named last changes fastest.
Arguments:
- inputs: bfloat16 [1, 16, 6144], P(None, 'et'), may hold values from -6 to 6
- cotangent: bfloat16 [1, 16, 6144], P(None, 'et'), may hold values from -6 to 6
- gate_weight: bfloat16 [2, 6144, 16384], P('segment', None, 'et'), may hold values from -0.078125 to 0.078125
- up_weight: bfloat16 [2, 6144, 16384], P('segment', None, 'et'), may hold values from -0.078125 to 0.078125
- down_weight: bfloat16 [2, 16384, 6144], P('segment', 'et'), may hold values from -0.0625 to 0.0625
- route_rows: int32 [2, 1, 16], P('segment'), may hold values from 0 to 15, as said below
- route_count: int32 [2, 1], P('segment'), may hold values from 4 to 16, as said below
- route_weight: float32 [2, 1, 16], P('segment'), may hold values from 0.05 to 1
- width_mask: int32 [2, 128], P('segment', 'et'), may hold values from 0 to 1, as said below
Outputs:
- section_output: bfloat16 [2, 1, 16, 6144], P('segment', None, 'et')
- grad_input: bfloat16 [2, 1, 16, 6144], P('segment', None, 'et')
- grad_gate: bfloat16 [2, 6144, 16384], P('segment', None, 'et')
- grad_up: bfloat16 [2, 6144, 16384], P('segment', None, 'et')
- grad_down: bfloat16 [2, 16384, 6144], P('segment', 'et')
Inputs may be any that keep to these rules, and one draw needn't show every extreme that they name: `route_rows`: each list names every one of the 16 tokens once; its first route_count entries are the slots routed to the expert. `route_count`: 16 in at least one entry. `width_mask`: the kept tiles of each section are its first ones, at least 32 of them and never all.
All inputs are finite; a program needn't handle non-finite values.
Results may differ from a plain program's by a relative error of at most 0.015.
Values may be sent and summed in bfloat16 or wider, within the bound.
A program may use at most 256 MiB of HBM per device.

v0:
```python
import jax
import jax.numpy as jnp
from jax import lax
from jax.sharding import PartitionSpec as P


def shifted(value, axis, by):
    size = lax.axis_size(axis)
    pairs = [(i, i + by) for i in range(size) if 0 <= i + by < size]
    return lax.ppermute(value, axis, pairs)


def expert_hidden(picked, gate_w, up_w, keep):
    gate_value = jnp.dot(picked, gate_w, preferred_element_type=jnp.float32)
    up_value = jnp.dot(picked, up_w, preferred_element_type=jnp.float32)
    hidden = (gate_value * jax.nn.sigmoid(gate_value) * up_value * keep).astype(jnp.bfloat16)
    return (gate_value, up_value, hidden)


def expert_deltas(picked, slot_grad_in, gate_value, up_value, hidden, down_w, keep):
    contract_last = (((1,), (1,)), ((), ()))
    contract_first = (((0,), (0,)), ((), ()))
    hidden_delta = lax.dot_general(
        slot_grad_in, down_w, contract_last, preferred_element_type=jnp.float32
    )
    sig_gate = jax.nn.sigmoid(gate_value)
    gate_delta = (
        hidden_delta * keep * up_value * sig_gate * (1.0 + gate_value * (1.0 - sig_gate))
    ).astype(jnp.bfloat16)
    up_delta = (hidden_delta * keep * gate_value * sig_gate).astype(jnp.bfloat16)
    grad_gate = lax.dot_general(
        picked, gate_delta, contract_first, preferred_element_type=jnp.float32
    )
    grad_up = lax.dot_general(picked, up_delta, contract_first, preferred_element_type=jnp.float32)
    grad_down = lax.dot_general(
        hidden, slot_grad_in, contract_first, preferred_element_type=jnp.float32
    )
    return (gate_delta, up_delta, grad_gate, grad_up, grad_down)


def slot_gradient(gate_delta, up_delta, gate_w, up_w):
    contract_last = (((1,), (1,)), ((), ()))
    slot_grad = lax.dot_general(
        gate_delta, gate_w, contract_last, preferred_element_type=jnp.float32
    )
    return slot_grad + lax.dot_general(
        up_delta, up_w, contract_last, preferred_element_type=jnp.float32
    )


def take_micro(buffer, micro_index):
    return lax.dynamic_index_in_dim(buffer, micro_index, 0, keepdims=False)


def store_micro(buffer, micro_index, value):
    return lax.dynamic_update_index_in_dim(buffer, value, micro_index, 0)


def pick_route(route_rows, route_count, route_weight, micro_index):
    slot_rows = take_micro(route_rows[0], micro_index)
    live_count = take_micro(route_count[0], micro_index)
    slot_weight = take_micro(route_weight[0], micro_index)
    slot_total = slot_rows.shape[0]
    positions = jnp.arange(slot_total, dtype=jnp.int32)
    live = positions < live_count
    inverse = jnp.zeros((slot_total,), jnp.int32).at[slot_rows].set(positions)
    return (slot_rows, jnp.where(live, slot_weight, 0.0), inverse)


def per_device(
    inputs,
    cotangent,
    gate_weight,
    up_weight,
    down_weight,
    route_rows,
    route_count,
    route_weight,
    width_mask,
):
    micro_count = inputs.shape[0]
    token_rows = inputs.shape[1]
    width = inputs.shape[2]
    segment_count = lax.axis_size("segment")
    segment_index = lax.axis_index("segment")
    total_rows = token_rows * lax.axis_size("et")
    slot_count = route_rows.shape[2]
    gate_w = gate_weight[0]
    up_w = up_weight[0]
    down_w = down_weight[0]
    hidden_cols = gate_w.shape[1]
    keep = jnp.repeat(width_mask[0].astype(jnp.float32), hidden_cols // width_mask.shape[1])
    phases = micro_count + segment_count - 1
    saved_input = jnp.zeros((micro_count, token_rows, width), jnp.bfloat16)
    saved_whole = jnp.zeros((micro_count, total_rows, width), jnp.bfloat16)
    saved_gate = jnp.zeros((micro_count, slot_count, hidden_cols), jnp.float32)
    saved_up = jnp.zeros((micro_count, slot_count, hidden_cols), jnp.float32)
    saved_hidden = jnp.zeros((micro_count, slot_count, hidden_cols), jnp.bfloat16)
    outputs = jnp.zeros((micro_count, token_rows, width), jnp.bfloat16)
    incoming = jnp.zeros((token_rows, width), jnp.bfloat16)
    for phase in range(phases):
        micro_raw = phase - segment_index
        valid = (micro_raw >= 0) & (micro_raw < micro_count)
        micro_index = jnp.clip(micro_raw, 0, micro_count - 1)
        current = jnp.where(segment_index == 0, take_micro(inputs, micro_index), incoming)
        gathered = lax.all_gather(current, "et", axis=0, tiled=True)
        slot_rows, slot_scale, inverse = pick_route(
            route_rows, route_count, route_weight, micro_index
        )
        picked = jnp.take(gathered, slot_rows, axis=0)
        gate_value, up_value, hidden = expert_hidden(picked, gate_w, up_w, keep)
        outcome = jnp.dot(hidden, down_w, preferred_element_type=jnp.float32)
        added = jnp.take(slot_scale[:, None] * outcome, inverse, axis=0)
        mine = lax.psum_scatter(added, "et", scatter_dimension=0, tiled=True)
        result = (current.astype(jnp.float32) + mine).astype(jnp.bfloat16)
        late = micro_raw >= 0
        stored = jnp.where(late, micro_index, micro_count - 1)
        saved_input = store_micro(saved_input, stored, current)
        saved_whole = store_micro(saved_whole, stored, gathered)
        saved_gate = store_micro(saved_gate, stored, gate_value)
        saved_up = store_micro(saved_up, stored, up_value)
        saved_hidden = store_micro(saved_hidden, stored, hidden)
        outputs = jnp.where(valid, store_micro(outputs, micro_index, result), outputs)
        if phase + 1 < phases:
            incoming = shifted(result, "segment", 1)
    acc_gate = jnp.zeros((width, hidden_cols), jnp.float32)
    acc_up = jnp.zeros((width, hidden_cols), jnp.float32)
    acc_down = jnp.zeros((hidden_cols, width), jnp.float32)
    grad_inputs = jnp.zeros((micro_count, token_rows, width), jnp.bfloat16)
    incoming = jnp.zeros((token_rows, width), jnp.bfloat16)
    for phase in range(phases):
        micro_raw = phase - (segment_count - 1 - segment_index)
        valid = (micro_raw >= 0) & (micro_raw < micro_count)
        micro_index = jnp.clip(micro_raw, 0, micro_count - 1)
        upstream = jnp.where(
            segment_index == segment_count - 1, take_micro(cotangent, micro_index), incoming
        )
        grad_gathered = lax.all_gather(upstream, "et", axis=0, tiled=True)
        gathered = take_micro(saved_whole, micro_index)
        slot_rows, slot_scale, inverse = pick_route(
            route_rows, route_count, route_weight, micro_index
        )
        slot_scale = jnp.where(valid, slot_scale, 0.0)
        picked = jnp.take(gathered, slot_rows, axis=0)
        grad_picked = jnp.take(grad_gathered, slot_rows, axis=0)
        slot_grad_in = (slot_scale[:, None] * grad_picked.astype(jnp.float32)).astype(jnp.bfloat16)
        gate_delta, up_delta, part_gate, part_up, part_down = expert_deltas(
            picked,
            slot_grad_in,
            take_micro(saved_gate, micro_index),
            take_micro(saved_up, micro_index),
            take_micro(saved_hidden, micro_index),
            down_w,
            keep,
        )
        acc_gate = acc_gate + part_gate
        acc_up = acc_up + part_up
        acc_down = acc_down + part_down
        slot_grad = slot_gradient(gate_delta, up_delta, gate_w, up_w)
        added = jnp.take(slot_grad, inverse, axis=0)
        mine = lax.psum_scatter(added, "et", scatter_dimension=0, tiled=True)
        result = (upstream.astype(jnp.float32) + mine).astype(jnp.bfloat16)
        grad_inputs = jnp.where(valid, store_micro(grad_inputs, micro_index, result), grad_inputs)
        if phase + 1 < phases:
            incoming = shifted(result, "segment", -1)
    return (
        outputs[None],
        grad_inputs[None],
        acc_gate.astype(jnp.bfloat16)[None],
        acc_up.astype(jnp.bfloat16)[None],
        acc_down.astype(jnp.bfloat16)[None],
    )


def solution(mesh):
    return jax.shard_map(
        per_device,
        mesh=mesh,
        in_specs=(
            P(None, "et", None),
            P(None, "et", None),
            P("segment", None, "et"),
            P("segment", None, "et"),
            P("segment", "et", None),
            P("segment", None, None),
            P("segment", None),
            P("segment", None, None),
            P("segment", "et"),
        ),
        out_specs=(
            P("segment", None, "et", None),
            P("segment", None, "et", None),
            P("segment", None, "et"),
            P("segment", None, "et"),
            P("segment", "et", None),
        ),
        check_vma=False,
    )
```

profile of v0, /device:TPU:0, one launch (start us, length us, event | category | flops | bytes accessed | tf_op | source)
XLA Modules:
  0.0 647.7 jit_solution(9052541303676647199)
XLA Ops:
  12.0 44.5 %all-gather = bf16[16,1,6144]{2,1,0:T(2,128)(2,1)S(1)} all-gather(bf16[1,1,6144]{2,1,0:T(2,128)(2,1)S(1)} %fusion.69), channel_id=1, replica_groups=mesh['segment'=2,'et'=16] {'et'}, dimensions={0}, use_global_device_ids=true | all-gather | bytes 208896 | tf_op jit(solution)/shard_map/all_gather | solution.py:106
  58.0 6.3 fusion.25
  64.3 11.6 %fusion.33 = f32[16,6144]{1,0:T(8,128)S(1)} fusion(bf16[1,1024,6144]{2,1,0:T(8,128)(2,1)} %param.17, bf16[1,6144,1024]{2,1,0:T(8,128)(2,1)} %param.16, f32[16]{0:T(128)S(1)} %get-tuple-element.10, bf16[16,6144]{1,0:T(8,128)(2,1)S(1)} %gather_fusion, pred[16]{0:T(512)(128)(4,1)S(1)} %compare_and_fusion.1, f32[16,1024]{1,0:T(8,128)S(1)} %fusion.25, ...), kind=kOutput, calls=%fused_computation.41 | convolution fusion | flops 402964480 | bytes 25825360 | tf_op jit(solution)/shard_map/dot_general | solution.py:112
  76.6 0.8 broadcast_select_fusion.3
  78.2 103.2 %all-reduce.9.cloned.1.call-done = f32[16,6144]{1,0:T(8,128)} async-done(((f32[16,6144]{1,0:T(8,128)}), f32[16,6144]{1,0:T(8,128)}) %all-reduce.9.cloned.1.call-update) | async-done | bytes 393232
  181.4 1.6 fusion.68
  183.0 1.3 collective-permute-start
  184.3 41.1 %all-gather.2 = bf16[16,1,6144]{2,1,0:T(2,128)(2,1)S(1)} all-gather(bf16[1,1,6144]{2,1,0:T(2,128)(2,1)S(1)} %fusion.70), channel_id=1, replica_groups=mesh['segment'=2,'et'=16] {'et'}, dimensions={0}, use_global_device_ids=true | all-gather | bytes 208896 | tf_op jit(solution)/shard_map/all_gather | solution.py:138
  226.3 37.7 %all-gather.1 = bf16[16,1,6144]{2,1,0:T(2,128)(2,1)S(1)} all-gather(bf16[1,1,6144]{2,1,0:T(2,128)(2,1)S(1)} %fusion.72), channel_id=1, replica_groups=mesh['segment'=2,'et'=16] {'et'}, dimensions={0}, use_global_device_ids=true | all-gather | bytes 208896 | tf_op jit(solution)/shard_map/all_gather | solution.py:106
  264.8 6.3 fusion.15
  271.1 6.4 fusion.23
  277.5 8.1 %multiply_convert_fusion.5 = (bf16[16,1024]{1,0:T(8,128)(2,1)S(1)}, bf16[16,1024]{1,0:T(8,128)(2,1)S(1)}) fusion(f32[16,1024]{1,0:T(8,128)S(1)} %fusion.15, f32[16,1024]{1,0:T(8,128)S(1)} %fusion.23, f32[1024]{0:T(1024)S(1)} %broadcast_bitcast_fusion, bf16[1,1024,6144]{2,1,0:T(8,128)(2,1)} %param.17, bf16[16,6144]{1,0:T(8,128)(2,1)S(1)} %gather_fusion.4, ...), kind=kOutput, calls=%fused_computation.63 | convolution fusion | flops 201949184 | bytes 12980304 | tf_op jit(solution)/shard_map/dot_general | solution.py:23
  285.6 8.1 %fusion.13 = f32[16,6144]{1,0:T(8,128)S(1)} fusion(bf16[16,1024]{1,0:T(8,128)(2,1)S(1)} %get-tuple-element.15, bf16[1,6144,1024]{2,1,0:T(8,128)(2,1)} %param.16), kind=kOutput, calls=%fused_computation.25 | convolution fusion | flops 201326592 | bytes 13008896 | tf_op jit(solution)/shard_map/dot_general | solution.py:46
  293.7 3.6 fusion.27
  298.0 0.8 broadcast_select_fusion.1
  298.9 10.2 %fusion.82 = f32[6144,1024]{1,0:T(8,128)} fusion(bf16[16,1024]{1,0:T(8,128)(2,1)S(1)} %get-tuple-element.14, bf16[16,6144]{1,0:T(8,128)(2,1)S(1)} %gather_fusion.2, pred[16]{0:T(512)(128)(4,1)S(1)} %compare_and_fusion.1), kind=kOutput, calls=%fused_computation.116 | convolution fusion | flops 201424896 | bytes 25395216 | tf_op jit(solution)/shard_map/dot_general | solution.py:31
  309.1 95.7 %all-reduce.11.cloned.1.call-done = f32[16,6144]{1,0:T(8,128)} async-done(((f32[16,6144]{1,0:T(8,128)}), f32[16,6144]{1,0:T(8,128)}) %all-reduce.11.cloned.1.call-update) | async-done | bytes 393232
  404.8 1.6 fusion.66
  406.4 1.3 collective-permute-start.1
  407.7 10.2 %fusion.81 = f32[6144,1024]{1,0:T(8,128)} fusion(bf16[16,1024]{1,0:T(8,128)(2,1)S(1)} %get-tuple-element.15, bf16[16,6144]{1,0:T(8,128)(2,1)S(1)} %gather_fusion.2, pred[16]{0:T(512)(128)(4,1)S(1)} %compare_and_fusion.1), kind=kOutput, calls=%fused_computation.115 | convolution fusion | flops 201424896 | bytes 25395216 | tf_op jit(solution)/shard_map/dot_general | solution.py:34
  417.9 41.2 %all-gather.3 = bf16[16,1,6144]{2,1,0:T(2,128)(2,1)S(1)} all-gather(bf16[1,1,6144]{2,1,0:T(2,128)(2,1)S(1)} %fusion.73), channel_id=1, replica_groups=mesh['segment'=2,'et'=16] {'et'}, dimensions={0}, use_global_device_ids=true | all-gather | bytes 208896 | tf_op jit(solution)/shard_map/all_gather | solution.py:138
  459.9 7.9 %multiply_convert_fusion.3 = (bf16[16,1024]{1,0:T(8,128)(2,1)S(1)}, bf16[16,1024]{1,0:T(8,128)(2,1)S(1)}, bf16[16,1024]{1,0:T(8,128)(2,1)S(1)}) fusion(f32[16,1024]{1,0:T(8,128)S(1)} %fusion.15, f32[16,1024]{1,0:T(8,128)S(1)} %fusion.23, f32[1024]{0:T(1024)S(1)} %broadcast_bitcast_fusion, bf16[1,1024,6144]{2,1,0:T(8,128)(2,1)} %param.17, ...), kind=kOutput, calls=%fused_computation.61 | convolution fusion | flops 202014720 | bytes 13013072 | tf_op jit(solution)/shard_map/dot_general | solution.py:23
  467.9 6.3 fusion.36
  474.2 10.4 %fusion.80 = f32[1024,6144]{1,0:T(8,128)} fusion(bf16[16,1024]{1,0:T(8,128)(2,1)S(1)} %get-tuple-element.12, bf16[16,6144]{1,0:T(8,128)(2,1)S(1)} %gather_fusion.4, f32[16]{0:T(128)S(1)} %broadcast_select_fusion.18, pred[16]{0:T(512)(128)(4,1)S(1)} %compare_and_fusion.1), kind=kOutput, calls=%fused_computation.114 | convolution fusion | flops 201719808 | bytes 25395280 | tf_op jit(solution)/shard_map/dot_general | solution.py:35
  485.3 7.9 %fusion.11 = f32[16,6144]{1,0:T(8,128)S(1)} fusion(bf16[16,1024]{1,0:T(8,128)(2,1)S(1)} %get-tuple-element.13, bf16[1,6144,1024]{2,1,0:T(8,128)(2,1)} %param.16), kind=kOutput, calls=%fused_computation.23 | convolution fusion | flops 201326592 | bytes 13008896 | tf_op jit(solution)/shard_map/dot_general | solution.py:46
  493.2 7.9 %fusion.30 = f32[16,6144]{1,0:T(8,128)S(1)} fusion(f32[16,6144]{1,0:T(8,128)S(1)} %fusion.11, bf16[16,1024]{1,0:T(8,128)(2,1)S(1)} %get-tuple-element.11, bf16[1,6144,1024]{2,1,0:T(8,128)(2,1)} %param.15), kind=kOutput, calls=%fused_computation.40 | convolution fusion | flops 201424896 | bytes 13402112 | tf_op jit(solution)/shard_map/dot_general | solution.py:43
  501.9 14.4 %fusion = bf16[1,6144,1024]{2,1,0:T(8,128)(2,1)} fusion(f32[6144,1024]{1,0:T(8,128)} %fusion.82, bf16[16,1024]{1,0:T(8,128)(2,1)S(1)} %get-tuple-element.11, bf16[16,6144]{1,0:T(8,128)(2,1)S(1)} %gather_fusion.2, pred[16]{0:T(512)(128)(4,1)S(1)} %compare_and_fusion.1), kind=kOutput, calls=%fused_computation.12 | convolution fusion | flops 214007808 | bytes 37978128 | tf_op jit(solution)/shard_map/dot_general | solution.py:31
  516.3 14.4 %fusion.1 = bf16[1,6144,1024]{2,1,0:T(8,128)(2,1)} fusion(f32[6144,1024]{1,0:T(8,128)} %fusion.81, bf16[16,1024]{1,0:T(8,128)(2,1)S(1)} %get-tuple-element.13, bf16[16,6144]{1,0:T(8,128)(2,1)S(1)} %gather_fusion.2, pred[16]{0:T(512)(128)(4,1)S(1)} %compare_and_fusion.1), kind=kOutput, calls=%fused_computation.13 | convolution fusion | flops 214007808 | bytes 37978128 | tf_op jit(solution)/shard_map/dot_general | solution.py:34
  530.7 1.0 broadcast_select_fusion
  531.7 14.8 %fusion.2 = bf16[1,1024,6144]{2,1,0:T(8,128)(2,1)} fusion(f32[1024,6144]{1,0:T(8,128)} %fusion.80, bf16[16,1024]{1,0:T(8,128)(2,1)S(1)} %get-tuple-element.12, bf16[16,6144]{1,0:T(8,128)(2,1)S(1)} %gather_fusion.6, f32[16]{0:T(128)S(1)} %get-tuple-element.9, pred[16]{0:T(512)(128)(4,1)S(1)} %compare_and_fusion.1), kind=kOutput, calls=%fused_computation.14 | convolution fusion | flops 214302720 | bytes 37978192 | tf_op jit(solution)/shard_map/dot_general | solution.py:35
  546.5 91.6 %all-reduce.13.cloned.1.call-done = (f32[16,6144]{1,0:T(8,128)}, f32[16,6144]{1,0:T(8,128)}) async-done(((f32[16,6144]{1,0:T(8,128)}, f32[16,6144]{1,0:T(8,128)}), (f32[16,6144]{1,0:T(8,128)}, f32[16,6144]{1,0:T(8,128)})) %all-reduce.13.cloned.1.call-update) | async-done | bytes 786448
  638.1 2.6 fusion.63
  (51 shorter events, 11.6 us)
Async XLA Ops:
  7.2 174.2 %all-reduce.9.cloned.1.call-start = ((), (), s32[]{:S(2)}) async-start(), calls=%async_computation | async-start | bytes 786432
  64.3 13.2 %copy-start.1 = (bf16[1,1,6144]{2,1,0:T(2,128)(2,1)S(1)}, bf16[1,1,6144]{2,1,0:T(2,128)(2,1)}, u32[]{:S(2)}) copy-start(bf16[1,1,6144]{2,1,0:T(2,128)(2,1)} %param.14) | copy-start | bytes 36868
  64.3 13.3 %copy-start.2 = (u32[32]{0:T(128)S(1)}, u32[32]{0:T(128)}, u32[]{:S(2)}) copy-start(u32[32]{0:T(128)} %constant.154) | copy-start | bytes 388
  64.3 117.1 %copy-start = (bf16[1,1,6144]{2,1,0:T(2,128)(2,1)S(1)}, bf16[1,1,6144]{2,1,0:T(2,128)(2,1)}, u32[]{:S(2)}) copy-start(bf16[1,1,6144]{2,1,0:T(2,128)(2,1)} %param.13) | copy-start | bytes 36868
  77.5 327.3 %all-reduce.11.cloned.1.call-start = ((), (), s32[]{:S(2)}) async-start(), calls=%async_computation.1 | async-start | bytes 786432
  183.0 43.2 %collective-permute-start = (bf16[1,6144]{1,0:T(2,128)(2,1)S(1)}, bf16[1,6144]{1,0:T(2,128)(2,1)S(1)}, u32[]{:S(2)}, u32[]{:S(2)}) collective-permute-start(bf16[1,6144]{1,0:T(2,128)(2,1)S(1)} %fusion.68), channel_id=1, source_target_pairs={{0,16},{1,17},{2,18},{3,19},{4,20},{5,21},{6,22},{7,23},{8,24},{9,... | collective-permute-start | bytes 36872 | tf_op jit(solution)/shard_map/ppermute | solution.py:10
  277.5 16.2 %slice-start = ((s8[12582912]{0:T(1024)(128)(4,1)}), s8[4194304]{0:T(1024)(128)(4,1)S(1)}, s32[]{:S(2)}) async-start(s8[12582912]{0:T(1024)(128)(4,1)} %bitcast.137), calls=%async_computation.3 | async-start | bytes 8388608
  277.5 16.2 %slice-start.1 = ((s8[12582912]{0:T(1024)(128)(4,1)}), s8[4194304]{0:T(1024)(128)(4,1)S(1)}, s32[]{:S(2)}) async-start(s8[12582912]{0:T(1024)(128)(4,1)} %bitcast.137), calls=%async_computation.4 | async-start | bytes 8388608
  285.6 8.1 %slice-start.2 = ((s8[12582912]{0:T(1024)(128)(4,1)}), s8[4194304]{0:T(1024)(128)(4,1)S(1)}, s32[]{:S(2)}) async-start(s8[12582912]{0:T(1024)(128)(4,1)} %bitcast.137), calls=%async_computation.5 | async-start | bytes 8388608
  298.8 339.3 %all-reduce.13.cloned.1.call-start = ((), (), s32[]{:S(2)}) async-start(), calls=%async_computation.2 | async-start | bytes 1572864
  406.4 11.5 %collective-permute-start.1 = (bf16[1,6144]{1,0:T(2,128)(2,1)S(1)}, bf16[1,6144]{1,0:T(2,128)(2,1)S(1)}, u32[]{:S(2)}, u32[]{:S(2)}) collective-permute-start(bf16[1,6144]{1,0:T(2,128)(2,1)S(1)} %fusion.66), channel_id=1, source_target_pairs={{16,0},{17,1},{18,2},{19,3},{20,4},{21,5},{22,6},{23,7},{24,8},{25... | collective-permute-start | bytes 36872 | tf_op jit(solution)/shard_map/ppermute | solution.py:10
Sparse Core Ops, SparseCore 0:
  77.6 103.7 all-reduce.8
  299.0 105.7 all-reduce.10
  531.8 106.2 all-reduce.12
where the time goes:
time: 654 us; the launch traced here: 648 us
  waiting for transfers between devices  291 us (44%)
  blocking collectives  164 us (25%)
  matrix products  155 us (24%)
  between operations  15.1 us (2%)
  other arithmetic  12.8 us (2%)
  local copies, waits for them, and re-layouts  7.2 us (1%)
    unnamed x6, waiting for transfers between devices  291 us
    all_gather x2, blocking collectives, per_device(): grad_gathered = lax.all_gather(upstream, 'et', axis=0, tiled=True)  82.3 us
    all_gather x2, blocking collectives, per_device(): gathered = lax.all_gather(current, 'et', axis=0, tiled=True)  82.2 us
    dot_general x2, matrix products, expert_deltas(): lax.dot_general(hidden, slot_grad_in, contract_first, preferred_element_t...  25.2 us
    dot_general x2, matrix products, expert_deltas(): lax.dot_general(picked, gate_delta, contract_first, preferred_element_typ...  24.6 us
    dot_general x2, matrix products, expert_deltas(): lax.dot_general(picked, up_delta, contract_first, preferred_element_type=...  24.6 us
    dot_general x2, matrix products, per_device(): outcome = jnp.dot(hidden, down_w, preferred_element_type=jnp.float32)  17.9 us
    dot_general x2, matrix products, expert_deltas(): lax.dot_general(slot_grad_in, down_w, contract_last, preferred_element_ty...  16 us
  transfers between devices with their start and end apart: 5, of which 3 were waited for; matrix products, arithmetic and copies ran while one was open for 6% of the time, Pallas kernels for 0%

commit v1 on v0

v1 whole, which is shorter than its diff:
```python
import functools
import jax
import jax.numpy as jnp
from jax import lax
from jax.experimental import pallas as pl
from jax.experimental.pallas import tpu as pltpu
from jax.sharding import PartitionSpec as P

MESH = pl.DeviceIdType.MESH
F32 = jnp.float32
BF16 = jnp.bfloat16
FOLD = 16
LAST = (((1,), (1,)), ((), ()))
FIRST = (((0,), (0,)), ((), ()))


def chunk_of(width):
    for size in (768, 512, 256, 128):
        if width % size == 0:
            return size
    return width


def chain_kernel(
    n,
    chunk,
    row_ref,
    scale_ref,
    keep_ref,
    gate_hbm,
    up_hbm,
    down_hbm,
    first_out,
    second_out,
    u_ref,
    sgi_ref,
    gd_ref,
    ud_ref,
    hid_ref,
    gate_w,
    up_w,
    down_w,
    first_all,
    second_all,
    send_a,
    send_b,
    recv_a,
    recv_b,
    fold_ref,
    part_ref,
    gate_val,
    up_val,
    load_sem,
    send_sem,
    recv_sem,
):
    seg = lax.axis_index("segment")
    me = lax.axis_index("et")
    other = 1 - seg
    width = u_ref.shape[1]
    hidden_cols = gate_w.shape[1]
    tokens = u_ref.shape[0]
    quota = width // FOLD
    steps = width // chunk

    def span(c):
        return pl.ds(pl.multiple_of(c * chunk, chunk), chunk)

    def load_gate(c):
        return pltpu.make_async_copy(gate_hbm.at[span(c)], gate_w.at[span(c)], load_sem.at[0, c])

    def load_up(c):
        return pltpu.make_async_copy(up_hbm.at[span(c)], up_w.at[span(c)], load_sem.at[1, c])

    def load_down(c):
        return pltpu.make_async_copy(
            down_hbm.at[:, span(c)], down_w.at[:, span(c)], load_sem.at[2, c]
        )

    @pl.when(seg == 0)
    def _():
        for c in range(steps):
            load_gate(c).start()
            load_up(c).start()
        for c in range(steps):
            load_down(c).start()

    @pl.when(seg == 1)
    def _():
        for c in range(steps):
            load_down(c).start()
        for c in range(steps):
            load_gate(c).start()
            load_up(c).start()

    barrier = pltpu.get_barrier_semaphore()

    def greet(k, _):
        pl.semaphore_signal(barrier, inc=1, device_id=(other, k), device_id_type=MESH)
        return 0

    def greet_own(k, _):
        pl.semaphore_signal(
            barrier, inc=1, device_id=(seg, lax.rem(me + k, n)), device_id_type=MESH
        )
        return 0

    lax.fori_loop(1, n, greet_own, 0)
    lax.fori_loop(0, n, greet, 0)
    pl.semaphore_wait(barrier, 2 * n - 1)

    def remote(src, dst, stage, to_seg, to_et):
        return pltpu.make_async_remote_copy(
            src_ref=src,
            dst_ref=dst,
            send_sem=send_sem.at[stage],
            recv_sem=recv_sem.at[stage],
            device_id=(to_seg, to_et),
            device_id_type=MESH,
        )

    def wait_bytes(buffer, count, sem):
        piece = buffer.at[pl.ds(0, count)]
        pltpu.make_async_copy(piece, piece, sem).wait()

    def send_first():
        def body(k, _):
            remote(row_ref, first_all.at[me], 0, seg, lax.rem(me + k, n)).start()
            return 0

        lax.fori_loop(1, n, body, 0)
        first_all[pl.ds(me, 1)] = row_ref[...][None]

    def send_second(src):
        def body(k, _):
            remote(src, second_all.at[me], 1, other, lax.rem(me + k, n)).start()
            return 0

        lax.fori_loop(0, n, body, 0)

    def unfold(buffer, out, scaled):
        fold_ref[...] = buffer[...].astype(F32)
        for j in range(FOLD):
            piece = fold_ref[:, j, :]
            if scaled:
                piece = piece * scale_ref[:, 0:1]
            out[:, j * quota : (j + 1) * quota] = piece.astype(BF16)

    def scatter(send, recv, stage):
        for j in range(FOLD):
            fold_ref[:, j, :] = part_ref[:, j * quota : (j + 1) * quota]
        send[...] = fold_ref[...].astype(BF16)

        def body(k, _):
            peer = lax.rem(me + k, n)
            remote(send.at[peer], recv.at[me], stage, seg, peer).start()
            return 0

        lax.fori_loop(1, n, body, 0)
        recv[pl.ds(me, 1)] = send[pl.ds(me, 1)]

    def gathered_sum(recv, stage):
        wait_bytes(recv, n - 1, recv_sem.at[stage])

        def body(k, total):
            return total + recv[k].astype(F32)

        return lax.fori_loop(0, n, body, jnp.zeros((FOLD, quota), F32))

    def project():
        def body(c, carry):
            gate_acc, up_acc = carry
            load_gate(c).wait()
            load_up(c).wait()
            rows = u_ref[:, span(c)]
            gate_acc = gate_acc + jnp.dot(rows, gate_w[span(c), :], preferred_element_type=F32)
            up_acc = up_acc + jnp.dot(rows, up_w[span(c), :], preferred_element_type=F32)
            return gate_acc, up_acc

        zero = jnp.zeros((tokens, hidden_cols), F32)
        gate_acc, up_acc = lax.fori_loop(0, steps, body, (zero, zero))
        gate_val[...] = gate_acc
        up_val[...] = up_acc
        hid_ref[...] = (gate_acc * jax.nn.sigmoid(gate_acc) * up_acc * keep_ref[...]).astype(BF16)

    def outcome(loads):
        def body(c, _):
            if loads:
                load_down(c).wait()
            value = jnp.dot(hid_ref[...], down_w[:, span(c)], preferred_element_type=F32)
            part_ref[:, span(c)] = value * scale_ref[:, 0:1]
            return 0

        lax.fori_loop(0, steps, body, 0)

    def hidden_delta(loads):
        def body(c, acc):
            if loads:
                load_down(c).wait()
            return acc + lax.dot_general(
                sgi_ref[:, span(c)], down_w[:, span(c)], LAST, preferred_element_type=F32
            )

        return lax.fori_loop(0, steps, body, jnp.zeros((tokens, hidden_cols), F32))

    def deltas(delta):
        gate_value = gate_val[...]
        sig = jax.nn.sigmoid(gate_value)
        kept = delta * keep_ref[...]
        gd_ref[...] = (kept * up_val[...] * sig * (1.0 + gate_value * (1.0 - sig))).astype(BF16)
        ud_ref[...] = (kept * gate_value * sig).astype(BF16)

    def slot_gradient():
        def body(c, _):
            value = lax.dot_general(
                gd_ref[...], gate_w[span(c), :], LAST, preferred_element_type=F32
            )
            part_ref[:, span(c)] = value + lax.dot_general(
                ud_ref[...], up_w[span(c), :], LAST, preferred_element_type=F32
            )
            return 0

        lax.fori_loop(0, steps, body, 0)

    send_first()

    @pl.when(seg == 0)
    def _():
        wait_bytes(first_all, n - 1, recv_sem.at[0])
        unfold(first_all, u_ref, False)
        project()
        outcome(True)
        scatter(send_a, recv_a, 2)
        total = gathered_sum(recv_a, 2)
        first_out[...] = (row_ref[...].astype(F32) + total).astype(BF16)
        send_second(first_out)
        wait_bytes(second_all, n, recv_sem.at[1])
        unfold(second_all, sgi_ref, True)
        deltas(hidden_delta(False))
        slot_gradient()
        scatter(send_b, recv_b, 3)
        total = gathered_sum(recv_b, 3)
        second_out[...] = (second_all[me].astype(F32) + total).astype(BF16)

    @pl.when(seg == 1)
    def _():
        wait_bytes(first_all, n - 1, recv_sem.at[0])
        unfold(first_all, sgi_ref, True)
        part_ref[:, 0:hidden_cols] = hidden_delta(True)
        wait_bytes(second_all, n, recv_sem.at[1])
        unfold(second_all, u_ref, False)
        project()
        deltas(part_ref[:, 0:hidden_cols])
        slot_gradient()
        scatter(send_a, recv_a, 2)
        total = gathered_sum(recv_a, 2)
        first_out[...] = (row_ref[...].astype(F32) + total).astype(BF16)
        send_second(first_out)
        outcome(False)
        scatter(send_b, recv_b, 3)
        total = gathered_sum(recv_b, 3)
        second_out[...] = (second_all[me].astype(F32) + total).astype(BF16)

    wait_bytes(first_all, n - 1, send_sem.at[0])
    wait_bytes(second_all, n, send_sem.at[1])
    wait_bytes(send_a, n - 1, send_sem.at[2])
    wait_bytes(send_b, n - 1, send_sem.at[3])


def chain(n, row, scale, keep, gate_w, up_w, down_w):
    tokens = scale.shape[0]
    width, hidden_cols = gate_w.shape
    quota = width // FOLD
    chunk = chunk_of(width)
    vmem = pl.BlockSpec(memory_space=pltpu.VMEM)
    hbm = pl.BlockSpec(memory_space=pl.ANY)
    shape = jax.ShapeDtypeStruct
    buffers = [pltpu.VMEM((n, FOLD, quota), BF16)] * 6
    return pl.pallas_call(
        functools.partial(chain_kernel, n, chunk),
        out_shape=(
            shape((FOLD, quota), BF16),
            shape((FOLD, quota), BF16),
            shape((tokens, width), BF16),
            shape((tokens, width), BF16),
            shape((tokens, hidden_cols), BF16),
            shape((tokens, hidden_cols), BF16),
            shape((tokens, hidden_cols), BF16),
        ),
        in_specs=[vmem, vmem, vmem, hbm, hbm, hbm],
        out_specs=(vmem,) * 7,
        scratch_shapes=[
            pltpu.VMEM((width, hidden_cols), BF16),
            pltpu.VMEM((width, hidden_cols), BF16),
            pltpu.VMEM((hidden_cols, width), BF16),
            *buffers,
            pltpu.VMEM((n, FOLD, quota), F32),
            pltpu.VMEM((tokens, width), F32),
            pltpu.VMEM((tokens, hidden_cols), F32),
            pltpu.VMEM((tokens, hidden_cols), F32),
            pltpu.SemaphoreType.DMA((3, width // chunk)),
            pltpu.SemaphoreType.DMA((4,)),
            pltpu.SemaphoreType.DMA((4,)),
        ],
        compiler_params=pltpu.CompilerParams(
            collective_id=0, has_side_effects=True, vmem_limit_bytes=56 * 1024 * 1024
        ),
        name="chain",
    )(row, scale, keep, gate_w, up_w, down_w)


def weights_kernel(u_ref, sgi_ref, gd_ref, ud_ref, hid_ref, gate_out, up_out, down_out):
    block, hidden_cols = gate_out.shape
    cols = min(256, hidden_cols)
    rows = min(128, block)
    for h in range(0, hidden_cols, cols):
        gate_delta = gd_ref[:, h : h + cols]
        up_delta = ud_ref[:, h : h + cols]
        for r in range(0, block, rows):
            picked = u_ref[:, r : r + rows]
            gate_out[r : r + rows, h : h + cols] = lax.dot_general(
                picked, gate_delta, FIRST, preferred_element_type=F32
            ).astype(BF16)
            up_out[r : r + rows, h : h + cols] = lax.dot_general(
                picked, up_delta, FIRST, preferred_element_type=F32
            ).astype(BF16)
    wide = min(256, block)
    for d in range(0, block, wide):
        slot_in = sgi_ref[:, d : d + wide]
        for h in range(0, hidden_cols, rows):
            down_out[h : h + rows, d : d + wide] = lax.dot_general(
                hid_ref[:, h : h + rows], slot_in, FIRST, preferred_element_type=F32
            ).astype(BF16)


def weight_gradients(u, sgi, gd, ud, hid):
    tokens, width = u.shape
    hidden_cols = gd.shape[1]
    block = 512 if width % 512 == 0 else width
    wide = pl.BlockSpec((tokens, block), lambda i: (0, i))
    whole = pl.BlockSpec((tokens, hidden_cols), lambda i: (0, 0))
    tall = pl.BlockSpec((block, hidden_cols), lambda i: (i, 0))
    shape = jax.ShapeDtypeStruct
    return pl.pallas_call(
        weights_kernel,
        grid=(width // block,),
        out_shape=(
            shape((width, hidden_cols), BF16),
            shape((width, hidden_cols), BF16),
            shape((hidden_cols, width), BF16),
        ),
        in_specs=[wide, wide, whole, whole, whole],
        out_specs=(tall, tall, pl.BlockSpec((hidden_cols, block), lambda i: (0, i))),
        compiler_params=pltpu.CompilerParams(vmem_limit_bytes=40 * 1024 * 1024),
        name="weight_gradients",
    )(u, sgi, gd, ud, hid)


def per_device(
    inputs,
    cotangent,
    gate_weight,
    up_weight,
    down_weight,
    route_rows,
    route_count,
    route_weight,
    width_mask,
):
    width = inputs.shape[2]
    n = lax.axis_size("et")
    seg = lax.axis_index("segment")
    slots = route_rows.shape[2]
    hidden_cols = gate_weight.shape[2]
    keep = jnp.repeat(width_mask.astype(F32), hidden_cols // width_mask.shape[1], axis=1)
    positions = jnp.arange(slots, dtype=jnp.int32)
    live = jnp.where(positions < route_count[0, 0], route_weight[0, 0], 0.0)
    hit = route_rows[0, 0][None, :] == positions[:, None]
    scale = jnp.sum(jnp.where(hit, live[None, :], 0.0), axis=1)
    scale = jnp.broadcast_to(scale[:, None], (slots, 128))
    row = jnp.where(seg == 0, inputs[0], cotangent[0]).reshape(FOLD, width // FOLD)
    first, second, u, sgi, gd, ud, hid = chain(
        n, row, scale, keep, gate_weight[0], up_weight[0], down_weight[0]
    )
    grad_gate, grad_up, grad_down = weight_gradients(u, sgi, gd, ud, hid)
    section = jnp.where(seg == 0, first, second).reshape(1, 1, 1, width)
    grad_in = jnp.where(seg == 0, second, first).reshape(1, 1, 1, width)
    return section, grad_in, grad_gate[None], grad_up[None], grad_down[None]


def solution(mesh):
    return jax.shard_map(
        per_device,
        mesh=mesh,
        in_specs=(
            P(None, "et", None),
            P(None, "et", None),
            P("segment", None, "et"),
            P("segment", None, "et"),
            P("segment", "et", None),
            P("segment", None, None),
            P("segment", None),
            P("segment", None, None),
            P("segment", "et"),
        ),
        out_specs=(
            P("segment", None, "et", None),
            P("segment", None, "et", None),
            P("segment", None, "et"),
            P("segment", None, "et"),
            P("segment", "et", None),
        ),
        check_vma=False,
    )
```

time: 654 us -> 101 us (0.15)
  waiting for transfers between devices: 291 us -> 0 us
  blocking collectives: 164 us -> 0 us
  matrix products: 155 us -> 0 us
  Pallas kernels: 0 us -> 87.7 us
  between operations: 15.1 us -> 1.31 us
  other arithmetic: 12.8 us -> 3.65 us
    unnamed x6 -> x0, waiting for transfers between devices: 291 us -> none
    all_gather x4 -> x0, blocking collectives: 164 us -> none  [the longest x2 82.3 us: per_device(): grad_gathered = lax.all_gather(upstream, 'et', axis=0, tiled=True)]
    dot_general x17 -> x0, matrix products: 155 us -> none  [the longest x2 25.2 us: expert_deltas(): lax.dot_general(hidden, slot_grad_in, contract_first, preferred_element_t...]
    pallas_call x0 -> x2, Pallas kernels: none -> 87.7 us  [the longest x1 72.2 us: chain(): pl.pallas_call(functools.partial(chain_kernel, n, chunk), out_shape=(shap...]
  transfers between devices with their start and end apart: 5 -> 0, of which waited for: 3 -> 0; matrix products, arithmetic and copies ran while one was open for 6% -> 0% of each run, Pallas kernels for 0% -> 0%
where the time goes in v1:
time: 101 us; the launch traced here: 100 us
  Pallas kernels  87.7 us (87%)
  local copies, waits for them, and re-layouts  7.31 us (7%)
  other arithmetic  3.65 us (4%)
  between operations  1.31 us (1%)
    pallas_call x1, Pallas kernels, chain(): pl.pallas_call(functools.partial(chain_kernel, n, chunk), out_shape=(shap...  72.2 us
    pallas_call x1, Pallas kernels, weight_gradients(): pl.pallas_call(weights_kernel, grid=(width // block,), out_shape=(shape((...  15.5 us
    unnamed x10, local copies, waits for them, and re-layouts  4.12 us

profile of v1, /device:TPU:0, one launch (start us, length us, event | category | flops | bytes accessed | tf_op | source)
XLA Modules:
  0.0 100.0 jit_solution(13003419409243759889)
XLA Ops:
  0.6 0.8 fusion
  1.5 0.6 select_n.41.row_ref
  2.7 0.7 compare_select_fusion
  3.4 0.8 select_reduce_fusion
  4.2 0.7 broadcast_in_dim.41.scale_ref
  4.8 0.7 convert_bitcast_fusion
  5.5 0.7 broadcast_in_dim.42
  6.2 72.2 %chain.1 = (bf16[16,384]{1,0:T(8,128)(2,1)}, bf16[16,384]{1,0:T(8,128)(2,1)}, bf16[16,6144]{1,0:T(8,128)(2,1)}, bf16[16,6144]{1,0:T(8,128)(2,1)}, bf16[16,1024]{...) custom-call(bf16[16,384]{1,0:T(8,128)(2,1)} %select_n.41.row_ref, ...), custom_call_target="tpu_custom_call" | custom-call | tf_op jit(solution)/shard_map/chain/pallas_call | solution.py:279
  78.4 0.0 copy-start
  78.4 0.9 copy-done
  79.3 0.0 copy-start.1
  79.3 0.9 copy-done.1
  80.2 0.0 copy-start.2
  80.2 0.8 copy-done.2
  81.0 0.0 copy-start.3
  81.0 0.8 copy-done.3
  81.7 0.0 copy-start.4
  81.7 0.8 copy-done.4
  82.5 15.5 %weight_gradients.1 = (bf16[6144,1024]{1,0:T(8,128)(2,1)}, bf16[6144,1024]{1,0:T(8,128)(2,1)}, bf16[1024,6144]{1,0:T(8,128)(2,1)}) custom-call(bf16[16,6144]{1,0:T(8,128)(2,1)S(1)} %copy-done, bf16[16,6144]{1,0:T(8,128)(2,1)S(1)} %copy-done.1, bf16[16,1024]{1,0:T(8,128)(2,1)S(1)} %copy-done.2, bf16[16,1024]{1,0:T(8,128)(2,1)S(1)} %copy-done.3, ...), custom_call_target="tpu_custom_call" | custom-call | tf_op jit(solution)/shard_map/weight_gradients/pallas_call | solution.py:344
  98.0 0.7 broadcast_select_fusion.1
  98.8 0.6 reshape.42
  99.4 0.6 reshape.43
Async XLA Ops:
  78.4 0.9 copy-start
  79.3 0.9 copy-start.1
  80.2 0.8 copy-start.2
  81.0 0.8 copy-start.3
  81.7 0.8 copy-start.4

commit v2 on v1

--- a/solution.py
+++ b/solution.py
@@ -15,7 +15,7 @@
 
 
 def chunk_of(width):
-    for size in (768, 512, 256, 128):
+    for size in (1536, 768, 512, 256, 128):
         if width % size == 0:
             return size
     return width
@@ -25,18 +25,16 @@
     n,
     chunk,
     row_ref,
-    scale_ref,
-    keep_ref,
+    rows_ref,
+    count_ref,
+    weight_ref,
+    mask_ref,
     gate_hbm,
     up_hbm,
     down_hbm,
     first_out,
     second_out,
-    u_ref,
-    sgi_ref,
-    gd_ref,
-    ud_ref,
-    hid_ref,
+    pack_ref,
     gate_w,
     up_w,
     down_w,
@@ -50,6 +48,8 @@
     part_ref,
     gate_val,
     up_val,
+    scale_ref,
+    keep_ref,
     load_sem,
     send_sem,
     recv_sem,
@@ -57,9 +57,13 @@
     seg = lax.axis_index("segment")
     me = lax.axis_index("et")
     other = 1 - seg
-    width = u_ref.shape[1]
-    hidden_cols = gate_w.shape[1]
-    tokens = u_ref.shape[0]
+    width, hidden_cols = gate_w.shape
+    tokens = pack_ref.shape[0]
+    u_ref = pack_ref.at[:, pl.ds(0, width)]
+    sgi_ref = pack_ref.at[:, pl.ds(width, width)]
+    gd_ref = pack_ref.at[:, pl.ds(2 * width, hidden_cols)]
+    ud_ref = pack_ref.at[:, pl.ds(2 * width + hidden_cols, hidden_cols)]
+    hid_ref = pack_ref.at[:, pl.ds(2 * width + 2 * hidden_cols, hidden_cols)]
     quota = width // FOLD
     steps = width // chunk
 
@@ -223,6 +227,18 @@
         lax.fori_loop(0, steps, body, 0)
 
     send_first()
+
+    slots = rows_ref.shape[1]
+    position = lax.broadcasted_iota(jnp.int32, (1, slots), 1)
+    live = jnp.where(position < count_ref[...], weight_ref[...], 0.0)
+    token = lax.broadcasted_iota(jnp.int32, (tokens, slots), 0)
+    hit = jnp.where(rows_ref[...] == token, live, 0.0)
+    scale_ref[...] = jnp.broadcast_to(jnp.sum(hit, axis=1, keepdims=True), scale_ref.shape)
+    tiles = mask_ref.shape[1]
+    tile = hidden_cols // tiles
+    for t in range(tiles):
+        kept = mask_ref[:, t : t + 1].astype(F32)
+        keep_ref[:, t * tile : (t + 1) * tile] = jnp.broadcast_to(kept, (1, tile))
 
     @pl.when(seg == 0)
     def _():
@@ -267,8 +283,8 @@
     wait_bytes(send_b, n - 1, send_sem.at[3])
 
 
-def chain(n, row, scale, keep, gate_w, up_w, down_w):
-    tokens = scale.shape[0]
+def chain(n, row, rows, count, weight, mask, gate_w, up_w, down_w):
+    tokens = n
     width, hidden_cols = gate_w.shape
     quota = width // FOLD
     chunk = chunk_of(width)
@@ -281,14 +297,10 @@
         out_shape=(
             shape((FOLD, quota), BF16),
             shape((FOLD, quota), BF16),
-            shape((tokens, width), BF16),
-            shape((tokens, width), BF16),
-            shape((tokens, hidden_cols), BF16),
-            shape((tokens, hidden_cols), BF16),
-            shape((tokens, hidden_cols), BF16),
+            shape((tokens, 2 * width + 3 * hidden_cols), BF16),
         ),
-        in_specs=[vmem, vmem, vmem, hbm, hbm, hbm],
-        out_specs=(vmem,) * 7,
+        in_specs=[vmem] * 5 + [hbm] * 3,
+        out_specs=(vmem,) * 3,
         scratch_shapes=[
             pltpu.VMEM((width, hidden_cols), BF16),
             pltpu.VMEM((width, hidden_cols), BF16),
@@ -298,6 +310,8 @@
             pltpu.VMEM((tokens, width), F32),
             pltpu.VMEM((tokens, hidden_cols), F32),
             pltpu.VMEM((tokens, hidden_cols), F32),
+            pltpu.VMEM((tokens, 128), F32),
+            pltpu.VMEM((1, hidden_cols), F32),
             pltpu.SemaphoreType.DMA((3, width // chunk)),
             pltpu.SemaphoreType.DMA((4,)),
             pltpu.SemaphoreType.DMA((4,)),
@@ -306,7 +320,7 @@
             collective_id=0, has_side_effects=True, vmem_limit_bytes=56 * 1024 * 1024
         ),
         name="chain",
-    )(row, scale, keep, gate_w, up_w, down_w)
+    )(row, rows, count, weight, mask, gate_w, up_w, down_w)
 
 
 def weights_kernel(u_ref, sgi_ref, gd_ref, ud_ref, hid_ref, gate_out, up_out, down_out):
@@ -333,12 +347,18 @@
             ).astype(BF16)
 
 
-def weight_gradients(u, sgi, gd, ud, hid):
-    tokens, width = u.shape
-    hidden_cols = gd.shape[1]
+def weight_gradients(pack, width, hidden_cols):
+    tokens = pack.shape[0]
     block = 512 if width % 512 == 0 else width
-    wide = pl.BlockSpec((tokens, block), lambda i: (0, i))
-    whole = pl.BlockSpec((tokens, hidden_cols), lambda i: (0, 0))
+    blocks = width // block
+    ahead = 2 * width // hidden_cols
+    specs = [
+        pl.BlockSpec((tokens, block), lambda i: (0, i)),
+        pl.BlockSpec((tokens, block), lambda i: (0, blocks + i)),
+        pl.BlockSpec((tokens, hidden_cols), lambda i: (0, ahead)),
+        pl.BlockSpec((tokens, hidden_cols), lambda i: (0, ahead + 1)),
+        pl.BlockSpec((tokens, hidden_cols), lambda i: (0, ahead + 2)),
+    ]
     tall = pl.BlockSpec((block, hidden_cols), lambda i: (i, 0))
     shape = jax.ShapeDtypeStruct
     return pl.pallas_call(
@@ -349,11 +369,11 @@
             shape((width, hidden_cols), BF16),
             shape((hidden_cols, width), BF16),
         ),
-        in_specs=[wide, wide, whole, whole, whole],
+        in_specs=specs,
         out_specs=(tall, tall, pl.BlockSpec((hidden_cols, block), lambda i: (0, i))),
         compiler_params=pltpu.CompilerParams(vmem_limit_bytes=40 * 1024 * 1024),
         name="weight_gradients",
-    )(u, sgi, gd, ud, hid)
+    )(pack, pack, pack, pack, pack)
 
 
 def per_device(
@@ -370,19 +390,20 @@
     width = inputs.shape[2]
     n = lax.axis_size("et")
     seg = lax.axis_index("segment")
-    slots = route_rows.shape[2]
     hidden_cols = gate_weight.shape[2]
-    keep = jnp.repeat(width_mask.astype(F32), hidden_cols // width_mask.shape[1], axis=1)
-    positions = jnp.arange(slots, dtype=jnp.int32)
-    live = jnp.where(positions < route_count[0, 0], route_weight[0, 0], 0.0)
-    hit = route_rows[0, 0][None, :] == positions[:, None]
-    scale = jnp.sum(jnp.where(hit, live[None, :], 0.0), axis=1)
-    scale = jnp.broadcast_to(scale[:, None], (slots, 128))
     row = jnp.where(seg == 0, inputs[0], cotangent[0]).reshape(FOLD, width // FOLD)
-    first, second, u, sgi, gd, ud, hid = chain(
-        n, row, scale, keep, gate_weight[0], up_weight[0], down_weight[0]
+    first, second, pack = chain(
+        n,
+        row,
+        route_rows[0],
+        route_count,
+        route_weight[0],
+        width_mask,
+        gate_weight[0],
+        up_weight[0],
+        down_weight[0],
     )
-    grad_gate, grad_up, grad_down = weight_gradients(u, sgi, gd, ud, hid)
+    grad_gate, grad_up, grad_down = weight_gradients(pack, width, hidden_cols)
     section = jnp.where(seg == 0, first, second).reshape(1, 1, 1, width)
     grad_in = jnp.where(seg == 0, second, first).reshape(1, 1, 1, width)
     return section, grad_in, grad_gate[None], grad_up[None], grad_down[None]

time: 101 us -> 90.4 us (0.90)
  local copies, waits for them, and re-layouts: 7.31 us -> 2.88 us
  Pallas kernels: 87.7 us -> 84.3 us
  other arithmetic: 3.65 us -> 1.57 us
    unnamed x10 -> x2, local copies, waits for them, and re-layouts: 4.12 us -> 1.03 us
    pallas_call x1, Pallas kernels: 72.2 us -> 69.2 us  [chain(): pl.pallas_call(functools.partial(chain_kernel, n, chunk), out_shape=(shap...]
    broadcast_in_dim x2 -> x0, local copies, waits for them, and re-layouts: 1.34 us -> none  [the longest x1 0.68 us: per_device(): scale = jnp.broadcast_to(scale[:, None], (slots, 128))]
where the time goes in v2:
time: 90.4 us; the launch traced here: 90 us
  Pallas kernels  84.3 us (93%)
  local copies, waits for them, and re-layouts  2.88 us (3%)
  other arithmetic  1.57 us (2%)
  between operations  1.29 us (1%)
    pallas_call x1, Pallas kernels, chain(): pl.pallas_call(functools.partial(chain_kernel, n, chunk), out_shape=(shap...  69.2 us
    pallas_call x1, Pallas kernels, weight_gradients(): pl.pallas_call(weights_kernel, grid=(width // block,), out_shape=(shape((...  15.1 us

profile of v2, /device:TPU:0, one launch (start us, length us, event | category | flops | bytes accessed | tf_op | source)
XLA Modules:
  0.0 90.0 jit_solution(12396044720795339694)
XLA Ops:
  1.3 0.8 fusion
  2.1 0.6 select_n.29.row_ref
  2.7 69.2 %chain.1 = (bf16[16,384]{1,0:T(8,128)(2,1)}, bf16[16,384]{1,0:T(8,128)(2,1)}, bf16[16,15360]{1,0:T(8,128)(2,1)}) custom-call(bf16[16,384]{1,0:T(8,128)(2,1)} %select_n.29.row_ref, s32[1,16]{1,0:T(1,128)} %bitcast.11, s32[1,1]{1,0:T(1,128)S(6)} %copy.14.count_ref, f32[1,16]{1,0:T(1,128)} %bitcast.12, s32[1,8]{1,0:T(1,128)} %mask_ref.1, ...), custom_call_target="tpu_custom_call" | custom-call | tf_op jit(solution)/shard_map/chain/pallas_call | solution.py:295
  71.9 0.7 broadcast_select_fusion.1
  72.6 0.6 reshape.27
  73.3 0.6 reshape.26
  73.9 0.0 copy-start
  73.9 1.0 %copy-done = bf16[16,15360]{1,0:T(8,128)(2,1)S(1)} copy-done((bf16[16,15360]{1,0:T(8,128)(2,1)S(1)}, bf16[16,15360]{1,0:T(8,128)(2,1)}, u32[]{:S(2)}) %copy-start) | copy-done | bytes 491544
  74.9 15.1 %weight_gradients.1 = (bf16[6144,1024]{1,0:T(8,128)(2,1)}, bf16[6144,1024]{1,0:T(8,128)(2,1)}, bf16[1024,6144]{1,0:T(8,128)(2,1)}) custom-call(bf16[16,15360]{1,0:T(8,128)(2,1)S(1)} %copy-done, bf16[16,15360]{1,0:T(8,128)(2,1)S(1)} %copy-done, bf16[16,15360]{1,0:T(8,128)(2,1)S(1)} %copy-done, bf16[16,15360]{1,0:T(8,128)(2,1)S(1)} %copy-done, ...), custom_call_target="tpu_custom_call" | custom-call | tf_op jit(solution)/shard_map/weight_gradients/pallas_call | solution.py:364
Async XLA Ops:
  73.9 1.0 %copy-start = (bf16[16,15360]{1,0:T(8,128)(2,1)S(1)}, bf16[16,15360]{1,0:T(8,128)(2,1)}, u32[]{:S(2)}) copy-start(bf16[16,15360]{1,0:T(8,128)(2,1)} %get-tuple-element.13.u_ref.sgi_ref.gd_ref.ud_ref.hid_ref) | copy-start | bytes 1474564

commit v3 on v2

--- a/solution.py
+++ b/solution.py
@@ -11,7 +11,6 @@
 BF16 = jnp.bfloat16
 FOLD = 16
 LAST = (((1,), (1,)), ((), ()))
-FIRST = (((0,), (0,)), ((), ()))
 
 
 def chunk_of(width):
@@ -32,8 +31,8 @@
     gate_hbm,
     up_hbm,
     down_hbm,
-    first_out,
-    second_out,
+    section_out,
+    grad_out,
     pack_ref,
     gate_w,
     up_w,
@@ -70,6 +69,11 @@
     def span(c):
         return pl.ds(pl.multiple_of(c * chunk, chunk), chunk)
 
+    big = 2 * chunk if steps % 2 == 0 else chunk
+
+    def big_span(c):
+        return pl.ds(pl.multiple_of(c * big, big), big)
+
     def load_gate(c):
         return pltpu.make_async_copy(gate_hbm.at[span(c)], gate_w.at[span(c)], load_sem.at[0, c])
 
@@ -199,13 +203,15 @@
 
     def hidden_delta(loads):
         def body(c, acc):
+            part = span(c) if loads else big_span(c)
             if loads:
                 load_down(c).wait()
             return acc + lax.dot_general(
-                sgi_ref[:, span(c)], down_w[:, span(c)], LAST, preferred_element_type=F32
+                sgi_ref[:, part], down_w[:, part], LAST, preferred_element_type=F32
             )
 
-        return lax.fori_loop(0, steps, body, jnp.zeros((tokens, hidden_cols), F32))
+        count = steps if loads else width // big
+        return lax.fori_loop(0, count, body, jnp.zeros((tokens, hidden_cols), F32))
 
     def deltas(delta):
         gate_value = gate_val[...]
@@ -217,14 +223,14 @@
     def slot_gradient():
         def body(c, _):
             value = lax.dot_general(
-                gd_ref[...], gate_w[span(c), :], LAST, preferred_element_type=F32
+                gd_ref[...], gate_w[big_span(c), :], LAST, preferred_element_type=F32
             )
-            part_ref[:, span(c)] = value + lax.dot_general(
-                ud_ref[...], up_w[span(c), :], LAST, preferred_element_type=F32
+            part_ref[:, big_span(c)] = value + lax.dot_general(
+                ud_ref[...], up_w[big_span(c), :], LAST, preferred_element_type=F32
             )
             return 0
 
-        lax.fori_loop(0, steps, body, 0)
+        lax.fori_loop(0, width // big, body, 0)
 
     send_first()
 
@@ -248,15 +254,15 @@
         outcome(True)
         scatter(send_a, recv_a, 2)
         total = gathered_sum(recv_a, 2)
-        first_out[...] = (row_ref[...].astype(F32) + total).astype(BF16)
-        send_second(first_out)
+        section_out[...] = (row_ref[...].astype(F32) + total).astype(BF16)
+        send_second(section_out)
         wait_bytes(second_all, n, recv_sem.at[1])
         unfold(second_all, sgi_ref, True)
         deltas(hidden_delta(False))
         slot_gradient()
         scatter(send_b, recv_b, 3)
         total = gathered_sum(recv_b, 3)
-        second_out[...] = (second_all[me].astype(F32) + total).astype(BF16)
+        grad_out[...] = (second_all[me].astype(F32) + total).astype(BF16)
 
     @pl.when(seg == 1)
     def _():
@@ -270,12 +276,12 @@
         slot_gradient()
         scatter(send_a, recv_a, 2)
         total = gathered_sum(recv_a, 2)
-        first_out[...] = (row_ref[...].astype(F32) + total).astype(BF16)
-        send_second(first_out)
+        grad_out[...] = (row_ref[...].astype(F32) + total).astype(BF16)
+        send_second(grad_out)
         outcome(False)
         scatter(send_b, recv_b, 3)
         total = gathered_sum(recv_b, 3)
-        second_out[...] = (second_all[me].astype(F32) + total).astype(BF16)
+        section_out[...] = (second_all[me].astype(F32) + total).astype(BF16)
 
     wait_bytes(first_all, n - 1, send_sem.at[0])
     wait_bytes(second_all, n, send_sem.at[1])
@@ -323,27 +329,39 @@
     )(row, rows, count, weight, mask, gate_w, up_w, down_w)
 
 
-def weights_kernel(u_ref, sgi_ref, gd_ref, ud_ref, hid_ref, gate_out, up_out, down_out):
+def turned(value):
+    return jnp.transpose(value.astype(F32)).astype(BF16)
+
+
+def weights_kernel(
+    u_ref, sgi_ref, gd_ref, ud_ref, hid_ref, gate_out, up_out, down_out, u_turned, hid_turned
+):
     block, hidden_cols = gate_out.shape
     cols = min(256, hidden_cols)
     rows = min(128, block)
+
+    @pl.when(pl.program_id(0) == 0)
+    def _():
+        hid_turned[...] = turned(hid_ref[...])
+
+    u_turned[...] = turned(u_ref[...])
     for h in range(0, hidden_cols, cols):
         gate_delta = gd_ref[:, h : h + cols]
         up_delta = ud_ref[:, h : h + cols]
         for r in range(0, block, rows):
-            picked = u_ref[:, r : r + rows]
-            gate_out[r : r + rows, h : h + cols] = lax.dot_general(
-                picked, gate_delta, FIRST, preferred_element_type=F32
+            picked = u_turned[r : r + rows, :]
+            gate_out[r : r + rows, h : h + cols] = jnp.dot(
+                picked, gate_delta, preferred_element_type=F32
             ).astype(BF16)
-            up_out[r : r + rows, h : h + cols] = lax.dot_general(
-                picked, up_delta, FIRST, preferred_element_type=F32
+            up_out[r : r + rows, h : h + cols] = jnp.dot(
+                picked, up_delta, preferred_element_type=F32
             ).astype(BF16)
     wide = min(256, block)
     for d in range(0, block, wide):
         slot_in = sgi_ref[:, d : d + wide]
         for h in range(0, hidden_cols, rows):
-            down_out[h : h + rows, d : d + wide] = lax.dot_general(
-                hid_ref[:, h : h + rows], slot_in, FIRST, preferred_element_type=F32
+            down_out[h : h + rows, d : d + wide] = jnp.dot(
+                hid_turned[h : h + rows, :], slot_in, preferred_element_type=F32
             ).astype(BF16)
 
 
@@ -371,6 +389,10 @@
         ),
         in_specs=specs,
         out_specs=(tall, tall, pl.BlockSpec((hidden_cols, block), lambda i: (0, i))),
+        scratch_shapes=[
+            pltpu.VMEM((block, tokens), BF16),
+            pltpu.VMEM((hidden_cols, tokens), BF16),
+        ],
         compiler_params=pltpu.CompilerParams(vmem_limit_bytes=40 * 1024 * 1024),
         name="weight_gradients",
     )(pack, pack, pack, pack, pack)
@@ -392,7 +414,7 @@
     seg = lax.axis_index("segment")
     hidden_cols = gate_weight.shape[2]
     row = jnp.where(seg == 0, inputs[0], cotangent[0]).reshape(FOLD, width // FOLD)
-    first, second, pack = chain(
+    section, grad_in, pack = chain(
         n,
         row,
         route_rows[0],
@@ -404,8 +426,8 @@
         down_weight[0],
     )
     grad_gate, grad_up, grad_down = weight_gradients(pack, width, hidden_cols)
-    section = jnp.where(seg == 0, first, second).reshape(1, 1, 1, width)
-    grad_in = jnp.where(seg == 0, second, first).reshape(1, 1, 1, width)
+    section = section.reshape(1, 1, 1, width)
+    grad_in = grad_in.reshape(1, 1, 1, width)
     return section, grad_in, grad_gate[None], grad_up[None], grad_down[None]
 
 

time: 90.4 us -> 90.8 us (level)
  local copies, waits for them, and re-layouts: 2.88 us -> 4.29 us
    reshape x2, local copies, waits for them, and re-layouts: 1.24 us -> 2.65 us  [the longest x1 1.32 us: per_device(): section = section.reshape(1, 1, 1, width)]
where the time goes in v3:
time: 90.8 us; the launch traced here: 90.4 us
  Pallas kernels  84 us (93%)
  local copies, waits for them, and re-layouts  4.29 us (5%)
  between operations  1.31 us (1%)
    pallas_call x1, Pallas kernels, chain(): pl.pallas_call(functools.partial(chain_kernel, n, chunk), out_shape=(shap...  68.5 us
    pallas_call x1, Pallas kernels, weight_gradients(): pl.pallas_call(weights_kernel, grid=(width // block,), out_shape=(shape((...  15.5 us

profile of v3, /device:TPU:0, one launch (start us, length us, event | category | flops | bytes accessed | tf_op | source)
XLA Modules:
  0.0 90.4 jit_solution(10805635431924970463)
XLA Ops:
  0.6 0.8 fusion
  1.5 0.6 select_n.16.row_ref
  2.7 68.5 %chain.1 = (bf16[16,384]{1,0:T(8,128)(2,1)}, bf16[16,384]{1,0:T(8,128)(2,1)}, bf16[16,15360]{1,0:T(8,128)(2,1)}) custom-call(bf16[16,384]{1,0:T(8,128)(2,1)} %select_n.16.row_ref, s32[1,16]{1,0:T(1,128)} %bitcast.11, s32[1,1]{1,0:T(1,128)S(6)} %copy.14.count_ref, f32[1,16]{1,0:T(1,128)} %bitcast.12, s32[1,8]{1,0:T(1,128)} %mask_ref.1, ...), custom_call_target="tpu_custom_call" | custom-call | tf_op jit(solution)/shard_map/chain/pallas_call | solution.py:301
  71.2 0.0 copy-start
  71.2 1.0 %copy-done = bf16[16,15360]{1,0:T(8,128)(2,1)S(1)} copy-done((bf16[16,15360]{1,0:T(8,128)(2,1)S(1)}, bf16[16,15360]{1,0:T(8,128)(2,1)}, u32[]{:S(2)}) %copy-start) | copy-done | bytes 491544
  72.2 15.5 %weight_gradients.1 = (bf16[6144,1024]{1,0:T(8,128)(2,1)}, bf16[6144,1024]{1,0:T(8,128)(2,1)}, bf16[1024,6144]{1,0:T(8,128)(2,1)}) custom-call(bf16[16,15360]{1,0:T(8,128)(2,1)S(1)} %copy-done, bf16[16,15360]{1,0:T(8,128)(2,1)S(1)} %copy-done, bf16[16,15360]{1,0:T(8,128)(2,1)S(1)} %copy-done, bf16[16,15360]{1,0:T(8,128)(2,1)S(1)} %copy-done, ...), custom_call_target="tpu_custom_call" | custom-call | tf_op jit(solution)/shard_map/weight_gradients/pallas_call | solution.py:382
  87.8 1.3 %reshape.26 = bf16[1,1,1,6144]{3,2,1,0:T(2,128)(2,1)} reshape(bf16[16,384]{1,0:T(8,128)(2,1)} %get-tuple-element.11) | data formatting | bytes 24576 | tf_op jit(solution)/shard_map/reshape | solution.py:429
  89.1 1.3 %reshape.27 = bf16[1,1,1,6144]{3,2,1,0:T(2,128)(2,1)} reshape(bf16[16,384]{1,0:T(8,128)(2,1)} %get-tuple-element.12) | data formatting | bytes 24576 | tf_op jit(solution)/shard_map/reshape | solution.py:430
Async XLA Ops:
  71.2 1.0 %copy-start = (bf16[16,15360]{1,0:T(8,128)(2,1)S(1)}, bf16[16,15360]{1,0:T(8,128)(2,1)}, u32[]{:S(2)}) copy-start(bf16[16,15360]{1,0:T(8,128)(2,1)} %get-tuple-element.13.u_ref.sgi_ref.gd_ref.ud_ref.hid_ref) | copy-start | bytes 1474564
